TPU v7x, 512 devices: a whole 4x4x16 slice. The times are simulated.
512 devices in a mesh: ia: 16 (over x, z_hi, core), ja: 32 (over y, z_lo).
Axes of the slice: x: 4, y: 4, z: 16 (z_hi: 2, z_lo: 8; z = z_hi * 8 + z_lo), core: 2. Of those that a mesh axis runs over, the one named last changes fastest.
Arguments:
- amplitudes: bfloat16 [64, 64, 64, 384], P('ia', 'ja'), may hold values from -6 to 6
- integrals: bfloat16 [64, 64, 64, 384], P('ja', 'ia'), may hold values from -0.078125 to 0.078125
Outputs:
- cycle_term: bfloat16 [64, 64, 4096], P('ia', 'ja')
All inputs are finite; a program needn't handle non-finite values.
Results may differ from a plain program's by a relative error of at most 0.0011.
Values may be sent and summed in bfloat16 or wider, within the bound.
A program may use at most 64 MiB of HBM per device.

v0:
```python
import jax
import jax.numpy as jnp
from jax import lax
from jax.sharding import PartitionSpec as P


def local(amplitudes, integrals):
    rows_i = amplitudes.shape[0]
    rows_k = amplitudes.shape[1]
    width = amplitudes.shape[2]
    total = rows_i * lax.axis_size("ia")
    first = lax.axis_index("ia") * rows_i
    direct = jnp.einsum(
        "ikac,kjbc->ijab",
        amplitudes,
        lax.all_gather(integrals, "ia", axis=1, tiled=True),
        preferred_element_type=jnp.float32,
    )
    summed = lax.psum_scatter(
        direct.reshape(rows_i, total, width * width), "ja", scatter_dimension=1, tiled=True
    )
    gathered = lax.all_gather(summed, "ia", axis=0, tiled=True)
    swapped = lax.all_to_all(gathered, "ja", split_axis=0, concat_axis=1, tiled=True)
    partner = lax.dynamic_slice_in_dim(swapped, first, rows_i, 1)
    partner = jnp.transpose(partner.reshape(rows_k, rows_i, width, width), (1, 0, 3, 2))
    return (summed + partner.reshape(rows_i, rows_k, width * width)).astype(jnp.bfloat16)


def solution(mesh):
    in_specs = (P("ia", "ja", None, None), P("ja", "ia", None, None))
    out_specs = P("ia", "ja", None)
    return jax.shard_map(local, mesh=mesh, in_specs=in_specs, out_specs=out_specs, check_vma=False)
```

profile of v0, /device:TPU:1, one launch (start us, length us, event | category | flops | bytes accessed | tf_op | source)
XLA Modules:
  0.0 867.8 jit_solution(14963908965752203708)
XLA Ops:
  6.5 0.0 copy-start
  6.5 0.0 all-gather.3.cloned.1.call-start
  6.5 1.8 copy.16
  8.4 0.0 all-gather.3.cloned.1.call-update
  8.4 0.0 all-reduce.3.cloned.1.call-start
  8.4 156.1 %all-gather.3.cloned.1.call-done = bf16[2,64,64,384]{3,2,0,1:T(8,128)(2,1)} async-done(((bf16[2,4,64,384]{3,2,0,1:T(8,128)(2,1)}), bf16[2,64,64,384]{3,2,0,1:T(8,128)(2,1)}) %all-gather.3.cloned.1.call-update) | async-done | bytes 6291472 | tf_op jit(solution)/shard_map/all_gather | solution.py:16
  164.6 0.0 copy-done
  164.6 7.7 fusion.2
  172.2 9.0 %copy.26 = f32[4,64,64,64]{3,2,0,1:T(8,128)} copy(f32[4,64,64,64]{2,3,0,1:T(8,128)} %fusion.2) | data formatting | bytes 8388608 | tf_op jit(solution)/shard_map/reshape | solution.py:20
  181.2 8.1 reshape.15
  189.3 0.0 all-reduce.3.cloned.1.call-update
  189.3 0.0 all-gather.5.cloned.1.call-start
  189.4 1.3 dynamic-slice
  191.3 456.1 %all-reduce.3.cloned.1.call-done = f32[4,64,4096]{2,0,1:T(4,128)} async-done(((f32[4,64,4096]{2,0,1:T(4,128)}), f32[4,64,4096]{2,0,1:T(4,128)}) %all-reduce.3.cloned.1.call-update) | async-done | bytes 4194320
  647.5 0.9 constant_dynamic-slice_fusion
  648.4 0.8 copy.23
  649.1 0.0 all-gather.5.cloned.1.call-update
  649.2 111.0 %all-gather.5.cloned.1.call-done = f32[64,2,4096]{2,1,0:T(2,128)} async-done(((f32[4,2,4096]{2,1,0:T(2,128)}), f32[64,2,4096]{2,1,0:T(2,128)}) %all-gather.5.cloned.1.call-update) | async-done | bytes 2097168 | tf_op jit(solution)/shard_map/all_gather | solution.py:22
  760.1 4.8 all-to-all-start
  764.9 92.6 %all-to-all-done = f32[64,2,4096]{2,1,0:T(2,128)S(1)} async-done(((f32[64,2,4096]{2,1,0:T(2,128)}), f32[64,2,4096]{2,1,0:T(2,128)S(1)}, u32[]{:S(2)}, u32[]{:S(2)}) %all-to-all-start) | async-done | bytes 2097184 | tf_op jit(solution)/shard_map/all_to_all | solution.py:23
  857.5 2.4 copy.20
  859.9 0.1 copy.21
  860.0 0.2 reshape.10
  860.2 0.1 copy.22
  860.3 0.1 reshape.11
  860.5 0.8 add_convert_fusion
  (1 shorter events, 0.0 us)
Async XLA Ops:
  6.5 158.0 %copy-start = (bf16[4,2,64,384]{3,2,1,0:T(8,128)(2,1)S(1)}, bf16[4,2,64,384]{3,2,1,0:T(8,128)(2,1)}, u32[]{:S(2)}) copy-start(bf16[4,2,64,384]{3,2,1,0:T(8,128)(2,1)} %param.2) | copy-start | bytes 1179652
  6.5 158.0 %all-gather.3.cloned.1.call-start = ((), (), s32[]{:S(2)}) async-start(), calls=%async_computation.1 | async-start | bytes 6684672 | tf_op jit(solution)/shard_map/all_gather | solution.py:16
  8.4 639.1 %all-reduce.3.cloned.1.call-start = ((), (), s32[]{:S(2)}) async-start(), calls=%async_computation.3 | async-start | bytes 8388608
  189.3 570.8 %all-gather.5.cloned.1.call-start = ((), (), s32[]{:S(2)}) async-start(), calls=%async_computation.2 | async-start | bytes 2228224 | tf_op jit(solution)/shard_map/all_gather | solution.py:22
  760.1 97.4 %all-to-all-start = ((f32[64,2,4096]{2,1,0:T(2,128)}), f32[64,2,4096]{2,1,0:T(2,128)S(1)}, u32[]{:S(2)}, u32[]{:S(2)}) async-start(f32[64,2,4096]{2,1,0:T(2,128)} %all-gather.5.cloned.1.call-done), calls=%async_computation | async-start | bytes 4194304 | tf_op jit(solution)/shard_map/all_to_all | solution.py:23
Sparse Core Ops, SparseCore 0:
  10.6 153.9 all-gather.2
  189.5 457.9 all-reduce.2
  650.7 109.3 all-gather.4
where the time goes:
time: 871 us; the launch traced here: 868 us
  waiting for transfers between devices  816 us (94%)
  local copies, waits for them, and re-layouts  24.8 us (3%)
  between operations  13.8 us (2%)
    unnamed x4, waiting for transfers between devices  456 us
    all_gather x1, waiting for transfers between devices, local(): lax.all_gather(integrals, 'ia', axis=1, tiled=True)  156 us
    all_gather x1, waiting for transfers between devices, local(): gathered = lax.all_gather(summed, 'ia', axis=0, tiled=True)  111 us
    all_to_all x1, waiting for transfers between devices, local(): lax.all_to_all(gathered, 'ja', split_axis=0, concat_axis=1, tiled=True)  92.6 us
  transfers between devices with their start and end apart: 4, of which 4 were waited for; matrix products, arithmetic and copies ran while one was open for 0% of the time, Pallas kernels for 0%

commit v1 on v0

v1 whole, which is shorter than its diff:
```python
import functools

import jax
import jax.numpy as jnp
from jax import lax
from jax.experimental import pallas as pl
from jax.experimental.pallas import tpu as pltpu
from jax.sharding import PartitionSpec as P

MESH = pl.DeviceIdType.MESH
F32 = jnp.float32


def place():
    ia, ja = lax.axis_index("ia"), lax.axis_index("ja")
    return ia // 4, ja // 8, (ia // 2) % 2, ja % 8, ia % 2


def device(x, y, zh, zl, c):
    return (x * 4 + zh * 2 + c, y * 8 + zl)


NAMES = (
    ["a1", "a2", "a3", "w"]
    + [f"{n}{r}{q}" for n in ("cross", "fwd") for r in range(2) for q in range(2)]
    + [f"{n}{s}" for n in ("m1p", "m1m", "m2p", "m2m", "m3p", "m3m", "z1", "z2") for s in range(4)]
    + [f"{n}{r}" for n in ("z4", "sw", "ta", "tb") for r in range(2)]
)
INDEX = {name: n for n, name in enumerate(NAMES)}


def kernel(a_ref, w_ref, o_ref, abuf, wbuf, t, m1, m2, m3, sum3, e, z1, f, z2, g, z4, gsum, drecv, rt, ss, rs, ls):
    x, y, zh, zl, c = place()
    b2, b1, b0 = zl // 4, (zl // 2) % 2, zl % 2
    keep = (b2 + zh) % 2
    diagonal = x == y
    local = jnp.logical_and(b2 == zh, b1 == c)

    def up(n, by):
        return (n + by) % 4

    a_to = [device(up(x, d), y, zh, zl, c) for d in (1, 2, 3)]
    sibling = device(x, y, zh, zl, 1 - c)
    anti = device(x, y, 1 - zh, zl, c)
    y_up, y_down = device(x, up(y, 1), zh, zl, c), device(x, up(y, 3), zh, zl, c)
    near = device(x, y, zh, b2 * 4 + b1 * 2 + 1 - b0, c)
    next_pair = device(x, y, zh, b2 * 4 + (1 - b1) * 2 + b0, c)
    far = device(x, y, zh, (1 - b2) * 4 + b1 * 2 + b0, c)
    swap = device(y, x, zh, zl, c)
    t_to = [device(x, y, b2, zh * 4 + c * 2 + q, b1) for q in range(2)]

    barrier = pltpu.get_barrier_semaphore()

    def greet(target):
        pl.semaphore_signal(barrier, inc=1, device_id=target, device_id_type=MESH)

    for target in a_to + [sibling, anti, y_up, y_down, near, next_pair, far]:
        greet(target)

    @pl.when(jnp.logical_not(diagonal))
    def _():
        greet(swap)

    for q in range(2):

        @pl.when(jnp.logical_not(jnp.logical_and(local, b0 == q)))
        def _():
            greet(t_to[q])

    pl.semaphore_wait(barrier, 12 + jnp.where(diagonal, 0, 1) - jnp.where(local, 1, 0))

    def copy(name, src, dst, target):
        n = INDEX[name]
        return pltpu.make_async_remote_copy(
            src_ref=src, dst_ref=dst, send_sem=ss.at[n], recv_sem=rs.at[n], device_id=target, device_id_type=MESH
        )

    cross = {}
    for r in range(2):
        for q in range(2):
            j = 2 * q + r
            cross[r, q] = copy(f"cross{r}{q}", w_ref.at[:, j], wbuf.at[1, c, :, j], anti)
            cross[r, q].start()
    sends = [copy(f"a{n + 1}", a_ref, abuf.at[x], a_to[n]) for n in range(3)]
    sends.append(copy("w", w_ref, wbuf.at[0, c], sibling))
    for one in sends:
        one.start()
    own_a = pltpu.make_async_copy(a_ref, abuf.at[x], ls.at[0])
    own_w = pltpu.make_async_copy(w_ref, wbuf.at[0, c], ls.at[1])
    own_a.start()
    own_w.start()
    own_a.wait()
    own_w.wait()
    for one in sends:
        one.wait()

    def product(s):
        sel, r = s // 2, s % 2

        def one(n, _):
            total = None
            for k in range(2):
                left = jnp.concatenate([wbuf[sel, cj, k, 2 * q + r] for cj in range(2) for q in range(2)], axis=0)
                right = abuf[n, :, k].reshape(256, 384)
                part = lax.dot_general(left, right, (((1,), (1,)), ((), ())), preferred_element_type=F32)
                total = part if total is None else total + part
            t[s, n] = total
            return 0

        lax.fori_loop(0, 4, one, 0)

    low, high = pl.ds(0, 128), pl.ds(128, 128)
    live = {}

    def begin(name, *rest):
        live[name] = copy(name, *rest)
        live[name].start()

    def y_start(s):
        begin(f"m1p{s}", t.at[s, up(y, 2), low], m1.at[s, 0], y_up)
        begin(f"m1m{s}", t.at[s, up(y, 2), high], m1.at[s, 1], y_down)
        begin(f"m2p{s}", t.at[s, up(y, 1), high], m2.at[s, 0], y_up)
        begin(f"m2m{s}", t.at[s, up(y, 3), low], m2.at[s, 1], y_down)

    def y_pass(s):
        live[f"m1p{s}"].wait()
        sum3[s, 0] = m1[s, 0] + t[s, up(y, 1), low]
        begin(f"m3p{s}", sum3.at[s, 0], m3.at[s, 0], y_up)
        live[f"m1m{s}"].wait()
        sum3[s, 1] = m1[s, 1] + t[s, up(y, 3), high]
        begin(f"m3m{s}", sum3.at[s, 1], m3.at[s, 1], y_down)

    def y_end(s):
        for name in ("m2p", "m2m", "m3p", "m3m"):
            live[f"{name}{s}"].wait()
        e[s, 0] = (t[s, y, low] + m3[s, 0] + m2[s, 1]).reshape(2, 64, 256)
        e[s, 1] = (t[s, y, high] + m2[s, 0] + m3[s, 1]).reshape(2, 64, 256)
        begin(f"z1{s}", e.at[s, :, 1 - b0], z1.at[s], near)

    def z_second(s):
        live[f"z1{s}"].wait()
        f[s] = e[s, :, b0] + z1[s]
        begin(f"z2{s}", f.at[s, 1 - b1], z2.at[s], next_pair)

    def z_third(s):
        sel, r = s // 2, s % 2
        live[f"z2{s}"].wait()
        g[r, sel] = f[s, b1] + z2[s]

        @pl.when(keep != sel)
        def _():
            copy(f"z4{r}", g.at[r, sel], z4.at[r], far).start()

    def last(r):
        copy(f"z4{r}", g.at[r, 0], z4.at[r], far).wait()
        gsum[r] = g[r, keep] + z4[r]

        @pl.when(diagonal)
        def _():
            drecv[r] = gsum[r]

        @pl.when(jnp.logical_not(diagonal))
        def _():
            copy(f"sw{r}", gsum.at[r], drecv.at[r], swap).start()

        for q in range(2):
            piece = gsum.at[r, :, pl.ds(q * 128, 128)]
            itself = jnp.logical_and(local, b0 == q)

            @pl.when(itself)
            def _():
                rt[b0, r] = piece[...]

            @pl.when(jnp.logical_not(itself))
            def _():
                n = INDEX[f"t{'ab'[q]}{r}"]
                pltpu.make_async_remote_copy(
                    src_ref=piece,
                    dst_ref=rt.at[b0, r],
                    send_sem=ss.at[n],
                    recv_sem=rs.at[INDEX[f"ta{r}"] + 2 * b0],
                    device_id=t_to[q],
                    device_id_type=MESH,
                ).start()

    def finish(r):
        @pl.when(jnp.logical_not(diagonal))
        def _():
            copy(f"sw{r}", gsum.at[r], drecv.at[r], swap).wait()

        for q in range(2):
            piece = gsum.at[r, :, pl.ds(q * 128, 128)]

            @pl.when(jnp.logical_not(jnp.logical_and(local, b0 == q)))
            def _():
                copy(f"t{'ab'[q]}{r}", piece, rt.at[q, r], t_to[q]).wait()

    def arrive(r):
        for q in range(2):
            j = 2 * q + r
            cross[r, q].wait()
            begin(f"fwd{r}{q}", wbuf.at[1, c, :, j], wbuf.at[1, c, :, j], sibling)

    def shared(r):
        for q in range(2):
            live[f"fwd{r}{q}"].wait()

    product(0)
    y_start(0)
    product(1)
    y_start(1)
    y_pass(0)
    y_pass(1)
    y_end(0)
    arrive(0)
    shared(0)
    product(2)
    y_start(2)
    y_end(1)
    z_second(0)
    z_second(1)
    y_pass(2)
    arrive(1)
    shared(1)
    product(3)
    y_start(3)
    z_third(0)
    z_third(1)
    y_end(2)
    y_pass(3)
    z_second(2)
    y_end(3)
    z_third(2)
    last(0)
    z_second(3)
    z_third(3)
    last(1)
    finish(0)
    finish(1)
    d = jnp.transpose(drecv[...].reshape(128, 256))
    o_ref[...] = (d + rt[...].reshape(256, 128)).astype(jnp.bfloat16)


def local(amplitudes, integrals):
    out = pl.pallas_call(
        kernel,
        out_shape=jax.ShapeDtypeStruct((256, 128), jnp.bfloat16),
        in_specs=[pl.BlockSpec(memory_space=pl.ANY)] * 2,
        out_specs=pl.BlockSpec(memory_space=pltpu.VMEM),
        scratch_shapes=[
            pltpu.VMEM((4, 4, 2, 64, 384), jnp.bfloat16),
            pltpu.VMEM((2, 2, 2, 4, 64, 384), jnp.bfloat16),
            pltpu.VMEM((4, 4, 256, 256), F32),
            pltpu.VMEM((4, 2, 128, 256), F32),
            pltpu.VMEM((4, 2, 128, 256), F32),
            pltpu.VMEM((4, 2, 128, 256), F32),
            pltpu.VMEM((4, 2, 128, 256), F32),
            pltpu.VMEM((4, 2, 2, 64, 256), F32),
            pltpu.VMEM((4, 2, 64, 256), F32),
            pltpu.VMEM((4, 2, 64, 256), F32),
            pltpu.VMEM((4, 64, 256), F32),
            pltpu.VMEM((2, 2, 64, 256), F32),
            pltpu.VMEM((2, 64, 256), F32),
            pltpu.VMEM((2, 64, 256), F32),
            pltpu.VMEM((2, 64, 256), F32),
            pltpu.VMEM((2, 2, 64, 128), F32),
            pltpu.SemaphoreType.DMA((len(NAMES),)),
            pltpu.SemaphoreType.DMA((len(NAMES),)),
            pltpu.SemaphoreType.DMA((2,)),
        ],
        compiler_params=pltpu.CompilerParams(
            collective_id=0, has_side_effects=True, vmem_limit_bytes=48 * 1024 * 1024
        ),
    )(amplitudes, integrals)
    out = jnp.transpose(out.reshape(4, 64, 2, 64), (0, 2, 1, 3))
    return out.reshape(4, 2, 4096)


def solution(mesh):
    in_specs = (P("ia", "ja", None, None), P("ja", "ia", None, None))
    out_specs = P("ia", "ja", None)
    return jax.shard_map(local, mesh=mesh, in_specs=in_specs, out_specs=out_specs, check_vma=False)
```

time: 871 us -> 104 us (0.12)
  waiting for transfers between devices: 816 us -> 0 us
  Pallas kernels: 0 us -> 101 us
  local copies, waits for them, and re-layouts: 24.8 us -> 2.91 us
  between operations: 13.8 us -> 0.03 us
    unnamed x4 -> x0, waiting for transfers between devices: 456 us -> none
    all_gather x2 -> x0, waiting for transfers between devices: 267 us -> none  [the longest x1 156 us: local(): lax.all_gather(integrals, 'ia', axis=1, tiled=True)]
    pallas_call x0 -> x1, Pallas kernels: none -> 101 us  [local(): pl.pallas_call(kernel, out_shape=jax.ShapeDtypeStruct((256, 128), jnp.bfl...]
    all_to_all x1 -> x0, waiting for transfers between devices: 92.6 us -> none  [local(): lax.all_to_all(gathered, 'ja', split_axis=0, concat_axis=1, tiled=True)]
    reshape x4 -> x2, local copies, waits for them, and re-layouts: 17.4 us -> 0.89 us  [the longest x1 0.8 us: local(): return out.reshape(4, 2, 4096)]
  transfers between devices with their start and end apart: 4 -> 0, of which waited for: 4 -> 0; matrix products, arithmetic and copies ran while one was open for 0% -> 0% of each run, Pallas kernels for 0% -> 0%
where the time goes in v1:
time: 104 us; the launch traced here: 103 us
  Pallas kernels  101 us (97%)
  local copies, waits for them, and re-layouts  2.91 us (3%)
    pallas_call x1, Pallas kernels, local(): pl.pallas_call(kernel, out_shape=jax.ShapeDtypeStruct((256, 128), jnp.bfl...  101 us

profile of v1, /device:TPU:1, one launch (start us, length us, event | category | flops | bytes accessed | tf_op | source)
XLA Modules:
  0.0 103.4 jit_solution(17969354235717784303)
XLA Ops:
  0.0 0.0 copy-start
  0.0 1.0 copy-done
  1.0 0.0 copy-start.1
  1.0 1.0 copy-done.1
  2.0 100.5 %shard_map.28 = bf16[256,128]{1,0:T(8,128)(2,1)S(1)} custom-call(bf16[4,2,64,384]{3,2,1,0:T(8,128)(2,1)S(1)} %copy-done, bf16[2,4,64,384]{3,2,1,0:T(8,128)(2,1)S(1)} %copy-done.1), custom_call_target="tpu_custom_call" | custom-call | tf_op jit(solution)/shard_map/pallas_call | solution.py:245
  102.5 0.1 reshape.6
  102.6 0.8 reshape.7
  (1 shorter events, 0.0 us)
Async XLA Ops:
  0.0 1.0 copy-start
  1.0 1.0 copy-start.1

commit v2 on v0

v2 whole, which is shorter than its diff:
```python
import jax
import jax.numpy as jnp
from jax import lax
from jax.experimental import pallas as pl
from jax.experimental.pallas import tpu as pltpu
from jax.sharding import PartitionSpec as P

MESH = pl.DeviceIdType.MESH
F32 = jnp.float32
ROWS = 16
PARTS = 64 // ROWS
STAGES = 2 * PARTS
AHEAD = 4
CAME = (24, 30, 36, 42)
READY = (27, 33, 39, 45)

NAMES = (
    ["a1", "a2", "a3", "w"]
    + [f"{n}{p}" for n in ("cross", "cf") for p in range(PARTS)]
    + [f"{n}{s}" for n in ("m1p", "m1m", "m2p", "m2m", "m3p", "m3m", "z1", "z2") for s in range(STAGES)]
    + [f"{n}{p}" for n in ("z4", "sw") for p in range(PARTS)]
    + [f"t{q}{p}" for p in range(PARTS) for q in range(2)]
)
INDEX = {name: n for n, name in enumerate(NAMES)}


LEVELS = 21
FINE = 10.4 * 256
TINY = 1e-30
CODED = True
WORDS, WORD = (3, jnp.bfloat16) if CODED else (2, jnp.float32)


def remainder(value, rounded):
    return jnp.round((value - rounded) * (FINE * pl.reciprocal(jnp.maximum(jnp.abs(rounded), TINY), approx=True)))


def encode(ref, first, second):
    if not CODED:
        ref[0], ref[1] = first, second
        return
    one, two = first.astype(jnp.bfloat16), second.astype(jnp.bfloat16)
    ref[0], ref[1] = one, two
    rest = remainder(first, one.astype(F32)) * LEVELS + remainder(second, two.astype(F32))
    ref[2] = rest.astype(jnp.bfloat16)


def decode(ref):
    if not CODED:
        return ref[0], ref[1]
    one, two, rest = ref[0].astype(F32), ref[1].astype(F32), ref[2].astype(F32)
    upper = jnp.round(rest * (1 / LEVELS))
    lower = rest - upper * LEVELS
    return one + upper * (jnp.abs(one) * (1 / FINE)), two + lower * (jnp.abs(two) * (1 / FINE))


def plan():
    steps = []
    for p in range(PARTS):
        for at, what in ((20 + 1.2 * p, "product"), (25 + 2.6 * p, "y_pass"), (29 + 2.8 * p, "y_end"),
                         (33 + 3 * p, "z_second"), (37 + 3 * p, "z_third")):
            steps.append((at, what, p))
        came = CAME[p]
        ready = READY[p]
        steps.append((came, "arrive", p))
        for offset, what in ((0, "product"), (5, "y_pass"), (9, "y_end"), (12.5, "z_second"), (16, "z_third")):
            steps.append((ready + offset, what, PARTS + p))
        steps.append((ready + 21, "last", p))
        steps.append((ready + 80, "finish", p))
    return [(what, n) for _, what, n in sorted(steps, key=lambda step: step[0])]


def kernel(a_ref, w_ref, o_ref, abuf, wbuf, t, y_out, y_in, e, z1_out, z1, f, z2_out, z2, g, z4_out, z4, gsum, drecv, rt, ss, rs, ls):
    ia, ja = lax.axis_index("ia"), lax.axis_index("ja")
    x, zh, c = ia // 4, (ia // 2) % 2, ia % 2
    y, zl = ja // 8, ja % 8
    b2, b1, b0 = zl // 4, (zl // 2) % 2, zl % 2
    keep = (b2 + zh) % 2

    def device(x, y, zh, zl, c):
        return (x * 4 + zh * 2 + c, y * 8 + zl)

    y_up, y_down = (y + 1) % 4, (y + 3) % 4

    sibling = device(x, y, zh, zl, 1 - c)
    a_to = [device((x + n) % 4, y, zh, zl, c) for n in (1, 3, 2)]
    anti = device(x, y, 1 - zh, zl, c)
    above, below = device(x, y_up, zh, zl, c), device(x, y_down, zh, zl, c)
    near = device(x, y, zh, b2 * 4 + b1 * 2 + 1 - b0, c)
    next_pair = device(x, y, zh, b2 * 4 + (1 - b1) * 2 + b0, c)
    far = device(x, y, zh, (1 - b2) * 4 + b1 * 2 + b0, c)

    swap = device(y, x, zh, zl, c)
    t_to = [device(x, y, b2, zh * 4 + c * 2 + q, b1) for q in range(2)]
    stays = x == y
    same = jnp.logical_and(b2 == zh, b1 == c)

    barrier = pltpu.get_barrier_semaphore()

    def greet(target):
        pl.semaphore_signal(barrier, inc=1, device_id=target, device_id_type=MESH)

    for target in (sibling, *a_to, anti, above, below, near, next_pair, far):
        greet(target)

    @pl.when(jnp.logical_not(stays))
    def _():
        greet(swap)

    for q in range(2):

        @pl.when(jnp.logical_not(jnp.logical_and(same, b0 == q)))
        def _():
            greet(t_to[q])

    pl.semaphore_wait(barrier, 13 - jnp.where(stays, 1, 0) - jnp.where(same, 1, 0))

    live = {}

    def copy(name, src, dst, target):
        n = INDEX[name]
        return pltpu.make_async_remote_copy(
            src_ref=src, dst_ref=dst, send_sem=ss.at[n], recv_sem=rs.at[n], device_id=target, device_id_type=MESH
        )

    def begin(name, *rest):
        live[name] = copy(name, *rest)
        live[name].start()

    def chunk(p):
        return pl.ds(p * ROWS, ROWS)

    def start_cross(p):
        begin(f"cross{p}", w_ref.at[:, :, chunk(p)], wbuf.at[1, c, :, :, chunk(p)], anti)

    for p in range(min(AHEAD, PARTS)):
        start_cross(p)
    for n in range(3):
        begin(f"a{n + 1}", a_ref, abuf.at[x], a_to[n])
    begin("w", w_ref, wbuf.at[0, c], sibling)
    own_a = pltpu.make_async_copy(a_ref, abuf.at[x], ls.at[0])
    own_w = pltpu.make_async_copy(w_ref, wbuf.at[0, c], ls.at[1])
    own_a.start()
    own_w.start()
    own_a.wait()
    own_w.wait()
    for name in ("w", "a1", "a2", "a3"):
        live[name].wait()

    def arrive(p):
        live[f"cross{p}"].wait()
        if p + AHEAD < PARTS:
            start_cross(p + AHEAD)
        part = wbuf.at[1, c, :, :, chunk(p)]
        begin(f"cf{p}", part, part, sibling)

    half = 4 * ROWS
    low, high = pl.ds(0, half), pl.ds(half, half)

    def product(s):
        sel, p = s // PARTS, s % PARTS
        if sel:
            live[f"cf{p}"].wait()

        def one(n, _):
            total = None
            for k in range(2):
                left = wbuf[sel, :, k, :, chunk(p)].reshape(8 * ROWS, 384)
                right = abuf[n, :, k].reshape(256, 384)
                part = lax.dot_general(left, right, (((1,), (1,)), ((), ())), preferred_element_type=F32)
                total = part if total is None else total + part
            t[s, n] = total
            return 0

        lax.fori_loop(0, 4, one, 0)
        y_send(s, 0, "m1p", t[s, (y + 2) % 4, low], above)
        y_send(s, 1, "m1m", t[s, (y + 2) % 4, high], below)
        y_send(s, 2, "m2p", t[s, y_up, high], above)
        y_send(s, 3, "m2m", t[s, y_down, low], below)

    def y_send(s, n, name, value, target):
        encode(y_out.at[s, n], value[: half // 2], value[half // 2 :])
        begin(f"{name}{s}", y_out.at[s, n], y_in.at[s, n], target)

    def y_got(s, n):
        return jnp.concatenate(decode(y_in.at[s, n]), axis=0)

    def y_pass(s):
        live[f"m1p{s}"].wait()
        y_send(s, 4, "m3p", y_got(s, 0) + t[s, y_up, low], above)
        live[f"m1m{s}"].wait()
        y_send(s, 5, "m3m", y_got(s, 1) + t[s, y_down, high], below)

    def y_end(s):
        for name in ("m2p", "m2m", "m3p", "m3m"):
            live[f"{name}{s}"].wait()
        e[s, 0] = (t[s, y, low] + y_got(s, 4) + y_got(s, 3)).reshape(2, 2 * ROWS, 256)
        e[s, 1] = (t[s, y, high] + y_got(s, 2) + y_got(s, 5)).reshape(2, 2 * ROWS, 256)
        encode(z1_out.at[s], e[s, 0, 1 - b0], e[s, 1, 1 - b0])
        begin(f"z1{s}", z1_out.at[s], z1.at[s], near)

    def z_second(s):
        live[f"z1{s}"].wait()
        got = decode(z1.at[s])
        f[s, 0] = e[s, 0, b0] + got[0]
        f[s, 1] = e[s, 1, b0] + got[1]
        encode(z2_out.at[s], f[s, 1 - b1, :ROWS], f[s, 1 - b1, ROWS:])
        begin(f"z2{s}", z2_out.at[s], z2.at[s], next_pair)

    def z_third(s):
        sel, p = s // PARTS, s % PARTS
        live[f"z2{s}"].wait()
        g[p, sel] = f[s, b1].reshape(2, ROWS, 256)
        got = decode(z2.at[s])
        g[p, sel, 0] += got[0]
        g[p, sel, 1] += got[1]

        @pl.when(keep != sel)
        def _():
            encode(z4_out.at[p], g[p, sel, 0], g[p, sel, 1])
            copy(f"z4{p}", z4_out.at[p], z4.at[p], far).start()

    def swapped(p):
        return copy(f"sw{p}", gsum.at[p], drecv.at[:, chunk(p)], swap)

    def last(p):
        copy(f"z4{p}", z4_out.at[p], z4.at[p], far).wait()
        got = decode(z4.at[p])
        gsum[p, 0] = g[p, keep, 0] + got[0]
        gsum[p, 1] = g[p, keep, 1] + got[1]

        @pl.when(stays)
        def _():
            drecv[:, chunk(p)] = gsum[p]

        @pl.when(jnp.logical_not(stays))
        def _():
            swapped(p).start()

        for q in range(2):
            itself = jnp.logical_and(same, b0 == q)

            @pl.when(itself)
            def _():
                rt[b0, :, chunk(p)] = gsum[p, :, :, q * 128 : (q + 1) * 128]

            @pl.when(jnp.logical_not(itself))
            def _():
                pltpu.make_async_remote_copy(
                    src_ref=gsum.at[p, :, :, pl.ds(q * 128, 128)],
                    dst_ref=rt.at[b0, :, chunk(p)],
                    send_sem=ss.at[INDEX[f"t{q}{p}"]],
                    recv_sem=rs.at[INDEX[f"t0{p}"] + b0],
                    device_id=t_to[q],
                    device_id_type=MESH,
                ).start()

    def finish(p):
        @pl.when(jnp.logical_not(stays))
        def _():
            swapped(p).wait()

        for q in range(2):

            @pl.when(jnp.logical_not(jnp.logical_and(same, b0 == q)))
            def _():
                copy(f"t{q}{p}", gsum.at[p, :, :, pl.ds(q * 128, 128)], rt.at[q, :, chunk(p)], t_to[q]).wait()

    what = dict(
        arrive=arrive, product=product, y_pass=y_pass, y_end=y_end, z_second=z_second, z_third=z_third,
        last=last, finish=finish,
    )
    for name, n in plan():
        what[name](n)
    d = jnp.transpose(drecv[...].reshape(128, 256))
    o_ref[...] = (d + rt[...].reshape(256, 128)).astype(jnp.bfloat16)


def local(amplitudes, integrals):
    out = pl.pallas_call(
        kernel,
        out_shape=jax.ShapeDtypeStruct((256, 128), jnp.bfloat16),
        in_specs=[pl.BlockSpec(memory_space=pltpu.HBM)] * 2,
        out_specs=pl.BlockSpec(memory_space=pltpu.VMEM),
        scratch_shapes=[
            pltpu.VMEM((4, 4, 2, 64, 384), jnp.bfloat16),
            pltpu.VMEM((2, 2, 2, 4, 64, 384), jnp.bfloat16),
            pltpu.VMEM((STAGES, 4, 8 * ROWS, 256), F32),
            pltpu.VMEM((STAGES, 6, WORDS, 2 * ROWS, 256), WORD),
            pltpu.VMEM((STAGES, 6, WORDS, 2 * ROWS, 256), WORD),
            pltpu.VMEM((STAGES, 2, 2, 2 * ROWS, 256), F32),
            pltpu.VMEM((STAGES, WORDS, 2 * ROWS, 256), WORD),
            pltpu.VMEM((STAGES, WORDS, 2 * ROWS, 256), WORD),
            pltpu.VMEM((STAGES, 2, 2 * ROWS, 256), F32),
            pltpu.VMEM((STAGES, WORDS, ROWS, 256), WORD),
            pltpu.VMEM((STAGES, WORDS, ROWS, 256), WORD),
            pltpu.VMEM((PARTS, 2, 2, ROWS, 256), F32),
            pltpu.VMEM((PARTS, WORDS, ROWS, 256), WORD),
            pltpu.VMEM((PARTS, WORDS, ROWS, 256), WORD),
            pltpu.VMEM((PARTS, 2, ROWS, 256), F32),
            pltpu.VMEM((2, 64, 256), F32),
            pltpu.VMEM((2, 2, 64, 128), F32),
            pltpu.SemaphoreType.DMA((len(NAMES),)),
            pltpu.SemaphoreType.DMA((len(NAMES),)),
            pltpu.SemaphoreType.DMA((2,)),
        ],
        compiler_params=pltpu.CompilerParams(
            collective_id=0, has_side_effects=True, vmem_limit_bytes=48 * 1024 * 1024
        ),
    )(amplitudes, integrals)
    out = jnp.transpose(out.reshape(4, 64, 2, 64), (0, 2, 1, 3))
    return out.reshape(4, 2, 4096)


def solution(mesh):
    in_specs = (P("ia", "ja", None, None), P("ja", "ia", None, None))
    out_specs = P("ia", "ja", None)
    return jax.shard_map(local, mesh=mesh, in_specs=in_specs, out_specs=out_specs, check_vma=False)
```

time: 871 us -> 91.5 us (0.11)
  waiting for transfers between devices: 816 us -> 0 us
  Pallas kernels: 0 us -> 88.3 us
  local copies, waits for them, and re-layouts: 24.8 us -> 2.91 us
  between operations: 13.8 us -> 0.03 us
    unnamed x4 -> x0, waiting for transfers between devices: 456 us -> none
    all_gather x2 -> x0, waiting for transfers between devices: 267 us -> none  [the longest x1 156 us: local(): lax.all_gather(integrals, 'ia', axis=1, tiled=True)]
    all_to_all x1 -> x0, waiting for transfers between devices: 92.6 us -> none  [local(): lax.all_to_all(gathered, 'ja', split_axis=0, concat_axis=1, tiled=True)]
    pallas_call x0 -> x1, Pallas kernels: none -> 88.3 us  [local(): pl.pallas_call(kernel, out_shape=jax.ShapeDtypeStruct((256, 128), jnp.bfl...]
    reshape x4 -> x2, local copies, waits for them, and re-layouts: 17.4 us -> 0.89 us  [the longest x1 0.8 us: local(): return out.reshape(4, 2, 4096)]
  transfers between devices with their start and end apart: 4 -> 0, of which waited for: 4 -> 0; matrix products, arithmetic and copies ran while one was open for 0% -> 0% of each run, Pallas kernels for 0% -> 0%
where the time goes in v2:
time: 91.5 us; the launch traced here: 91.2 us
  Pallas kernels  88.3 us (97%)
  local copies, waits for them, and re-layouts  2.91 us (3%)
    pallas_call x1, Pallas kernels, local(): pl.pallas_call(kernel, out_shape=jax.ShapeDtypeStruct((256, 128), jnp.bfl...  88.3 us
    unnamed x4, local copies, waits for them, and re-layouts  1.99 us

profile of v2, /device:TPU:1, one launch (start us, length us, event | category | flops | bytes accessed | tf_op | source)
XLA Modules:
  0.0 91.2 jit_solution(3646625513848220761)
XLA Ops:
  0.0 0.0 copy-start
  0.0 1.0 %copy-done = bf16[4,2,64,384]{3,2,1,0:T(8,128)(2,1)S(1)} copy-done((bf16[4,2,64,384]{3,2,1,0:T(8,128)(2,1)S(1)}, bf16[4,2,64,384]{3,2,1,0:T(8,128)(2,1)}, u32[]{:S(2)}) %copy-start) | copy-done | bytes 393240
  1.0 0.0 copy-start.1
  1.0 1.0 %copy-done.1 = bf16[2,4,64,384]{3,2,1,0:T(8,128)(2,1)S(1)} copy-done((bf16[2,4,64,384]{3,2,1,0:T(8,128)(2,1)S(1)}, bf16[2,4,64,384]{3,2,1,0:T(8,128)(2,1)}, u32[]{:S(2)}) %copy-start.1) | copy-done | bytes 393240
  2.0 88.3 %shard_map.28 = bf16[256,128]{1,0:T(8,128)(2,1)S(1)} custom-call(bf16[4,2,64,384]{3,2,1,0:T(8,128)(2,1)S(1)} %copy-done, bf16[2,4,64,384]{3,2,1,0:T(8,128)(2,1)S(1)} %copy-done.1), custom_call_target="tpu_custom_call" | custom-call | tf_op jit(solution)/shard_map/pallas_call | solution.py:280
  90.3 0.1 reshape.6
  90.4 0.8 reshape.7
  (1 shorter events, 0.0 us)
Async XLA Ops:
  0.0 1.0 %copy-start = (bf16[4,2,64,384]{3,2,1,0:T(8,128)(2,1)S(1)}, bf16[4,2,64,384]{3,2,1,0:T(8,128)(2,1)}, u32[]{:S(2)}) copy-start(bf16[4,2,64,384]{3,2,1,0:T(8,128)(2,1)} %a_ref.1) | copy-start | bytes 1179652
  1.0 1.0 %copy-start.1 = (bf16[2,4,64,384]{3,2,1,0:T(8,128)(2,1)S(1)}, bf16[2,4,64,384]{3,2,1,0:T(8,128)(2,1)}, u32[]{:S(2)}) copy-start(bf16[2,4,64,384]{3,2,1,0:T(8,128)(2,1)} %w_ref.1) | copy-start | bytes 1179652

commit v3 on v2

--- a/solution.py
+++ b/solution.py
@@ -10,14 +10,14 @@
 ROWS = 16
 PARTS = 64 // ROWS
 STAGES = 2 * PARTS
+DIRECT = (6, 7)
 AHEAD = 4
-CAME = (24, 30, 36, 42)
-READY = (27, 33, 39, 45)
+CAME = (22, 28, 34, 40)
 
 NAMES = (
     ["a1", "a2", "a3", "w"]
     + [f"{n}{p}" for n in ("cross", "cf") for p in range(PARTS)]
-    + [f"{n}{s}" for n in ("m1p", "m1m", "m2p", "m2m", "m3p", "m3m", "z1", "z2") for s in range(STAGES)]
+    + [f"{n}{s}" for n in ("y0", "y1", "y2", "y3", "y4", "y5", "z1", "z2", "z3") for s in range(STAGES)]
     + [f"{n}{p}" for n in ("z4", "sw") for p in range(PARTS)]
     + [f"t{q}{p}" for p in range(PARTS) for q in range(2)]
 )
@@ -57,20 +57,20 @@
 def plan():
     steps = []
     for p in range(PARTS):
-        for at, what in ((20 + 1.2 * p, "product"), (25 + 2.6 * p, "y_pass"), (29 + 2.8 * p, "y_end"),
-                         (33 + 3 * p, "z_second"), (37 + 3 * p, "z_third")):
+        for at, what in ((20 + 1.2 * p, "product"), (26 + 3.5 * p, "y_pass"), (32 + 3.5 * p, "y_end"), (37 + 3.5 * p, "z_end")):
             steps.append((at, what, p))
-        came = CAME[p]
-        ready = READY[p]
-        steps.append((came, "arrive", p))
-        for offset, what in ((0, "product"), (5, "y_pass"), (9, "y_end"), (12.5, "z_second"), (16, "z_third")):
-            steps.append((ready + offset, what, PARTS + p))
-        steps.append((ready + 21, "last", p))
-        steps.append((ready + 80, "finish", p))
+        steps.append((CAME[p], "arrive", p))
+        ready, offsets = CAME[p] + 3, (5, 9, 17) if PARTS + p in DIRECT else (9, 13, 21)
+        steps.append((ready, "product", PARTS + p))
+        steps.append((ready + 5.05, "y_pass", PARTS + p))
+        steps.append((ready + offsets[0], "y_end", PARTS + p))
+        steps.append((ready + offsets[1], "z_end", PARTS + p))
+        steps.append((max(ready + offsets[2], 37.1 + 3.5 * p), "last", p))
+        steps.append((ready + 100, "finish", p))
     return [(what, n) for _, what, n in sorted(steps, key=lambda step: step[0])]
 
 
-def kernel(a_ref, w_ref, o_ref, abuf, wbuf, t, y_out, y_in, e, z1_out, z1, f, z2_out, z2, g, z4_out, z4, gsum, drecv, rt, ss, rs, ls):
+def kernel(a_ref, w_ref, o_ref, abuf, wbuf, t, y_out, y_in, e, z_out, z_in, g, z4_out, z4, gsum, drecv, rt, ss, rs, ls):
     ia, ja = lax.axis_index("ia"), lax.axis_index("ja")
     x, zh, c = ia // 4, (ia // 2) % 2, ia % 2
     y, zl = ja // 8, ja % 8
@@ -80,14 +80,13 @@
     def device(x, y, zh, zl, c):
         return (x * 4 + zh * 2 + c, y * 8 + zl)
 
-    y_up, y_down = (y + 1) % 4, (y + 3) % 4
 
     sibling = device(x, y, zh, zl, 1 - c)
     a_to = [device((x + n) % 4, y, zh, zl, c) for n in (1, 3, 2)]
     anti = device(x, y, 1 - zh, zl, c)
-    above, below = device(x, y_up, zh, zl, c), device(x, y_down, zh, zl, c)
-    near = device(x, y, zh, b2 * 4 + b1 * 2 + 1 - b0, c)
-    next_pair = device(x, y, zh, b2 * 4 + (1 - b1) * 2 + b0, c)
+    y_to = [device(x, (y + n) % 4, zh, zl, c) for n in range(4)]
+    quad = [(b1, b0), (b1, 1 - b0), (1 - b1, b0), (1 - b1, 1 - b0)]
+    z_to = [device(x, y, zh, b2 * 4 + two * 2 + one, c) for two, one in quad]
     far = device(x, y, zh, (1 - b2) * 4 + b1 * 2 + b0, c)
 
     swap = device(y, x, zh, zl, c)
@@ -100,7 +99,7 @@
     def greet(target):
         pl.semaphore_signal(barrier, inc=1, device_id=target, device_id_type=MESH)
 
-    for target in (sibling, *a_to, anti, above, below, near, next_pair, far):
+    for target in (sibling, anti, far, *a_to, *y_to[1:], *z_to[1:]):
         greet(target)
 
     @pl.when(jnp.logical_not(stays))
@@ -113,7 +112,7 @@
         def _():
             greet(t_to[q])
 
-    pl.semaphore_wait(barrier, 13 - jnp.where(stays, 1, 0) - jnp.where(same, 1, 0))
+    pl.semaphore_wait(barrier, 15 - jnp.where(stays, 1, 0) - jnp.where(same, 1, 0))
 
     live = {}
 
@@ -154,8 +153,7 @@
         part = wbuf.at[1, c, :, :, chunk(p)]
         begin(f"cf{p}", part, part, sibling)
 
-    half = 4 * ROWS
-    low, high = pl.ds(0, half), pl.ds(half, half)
+    low, high = pl.ds(0, 4 * ROWS), pl.ds(4 * ROWS, 4 * ROWS)
 
     def product(s):
         sel, p = s // PARTS, s % PARTS
@@ -173,47 +171,52 @@
             return 0
 
         lax.fori_loop(0, 4, one, 0)
-        y_send(s, 0, "m1p", t[s, (y + 2) % 4, low], above)
-        y_send(s, 1, "m1m", t[s, (y + 2) % 4, high], below)
-        y_send(s, 2, "m2p", t[s, y_up, high], above)
-        y_send(s, 3, "m2m", t[s, y_down, low], below)
-
-    def y_send(s, n, name, value, target):
-        encode(y_out.at[s, n], value[: half // 2], value[half // 2 :])
-        begin(f"{name}{s}", y_out.at[s, n], y_in.at[s, n], target)
+        direct = s in DIRECT
+        y_send(s, 0, t[s, (y + 2) % 4, low], y_to[2 if direct else 1])
+        y_send(s, 1, t[s, (y + 2) % 4, high], y_to[2 if direct else 3])
+        y_send(s, 2, t[s, (y + 1) % 4, high], y_to[1])
+        y_send(s, 3, t[s, (y + 3) % 4, low], y_to[3])
+        if direct:
+            y_send(s, 4, t[s, (y + 1) % 4, low], y_to[1])
+            y_send(s, 5, t[s, (y + 3) % 4, high], y_to[3])
+
+    def y_send(s, n, value, target):
+        encode(y_out.at[s, n], value[: 2 * ROWS], value[2 * ROWS :])
+        begin(f"y{n}{s}", y_out.at[s, n], y_in.at[s, n], target)
 
     def y_got(s, n):
+        live[f"y{n}{s}"].wait()
         return jnp.concatenate(decode(y_in.at[s, n]), axis=0)
 
     def y_pass(s):
-        live[f"m1p{s}"].wait()
-        y_send(s, 4, "m3p", y_got(s, 0) + t[s, y_up, low], above)
-        live[f"m1m{s}"].wait()
-        y_send(s, 5, "m3m", y_got(s, 1) + t[s, y_down, high], below)
+        if s not in DIRECT:
+            y_send(s, 4, y_got(s, 0) + t[s, (y + 1) % 4, low], y_to[1])
+            y_send(s, 5, y_got(s, 1) + t[s, (y + 3) % 4, high], y_to[3])
 
     def y_end(s):
-        for name in ("m2p", "m2m", "m3p", "m3m"):
-            live[f"{name}{s}"].wait()
-        e[s, 0] = (t[s, y, low] + y_got(s, 4) + y_got(s, 3)).reshape(2, 2 * ROWS, 256)
-        e[s, 1] = (t[s, y, high] + y_got(s, 2) + y_got(s, 5)).reshape(2, 2 * ROWS, 256)
-        encode(z1_out.at[s], e[s, 0, 1 - b0], e[s, 1, 1 - b0])
-        begin(f"z1{s}", z1_out.at[s], z1.at[s], near)
-
-    def z_second(s):
-        live[f"z1{s}"].wait()
-        got = decode(z1.at[s])
-        f[s, 0] = e[s, 0, b0] + got[0]
-        f[s, 1] = e[s, 1, b0] + got[1]
-        encode(z2_out.at[s], f[s, 1 - b1, :ROWS], f[s, 1 - b1, ROWS:])
-        begin(f"z2{s}", z2_out.at[s], z2.at[s], next_pair)
-
-    def z_third(s):
+        first = t[s, y, low] + y_got(s, 3)
+        second = t[s, y, high] + y_got(s, 2)
+        if s in DIRECT:
+            first += y_got(s, 0)
+            second += y_got(s, 1)
+        first += y_got(s, 4)
+        second += y_got(s, 5)
+        e[s, 0] = first.reshape(2, 2, ROWS, 256)
+        e[s, 1] = second.reshape(2, 2, ROWS, 256)
+        for n in (3, 2, 1):
+            two, one = quad[n]
+            encode(z_out.at[s, n - 1], e[s, two, one, 0], e[s, two, one, 1])
+            begin(f"z{n}{s}", z_out.at[s, n - 1], z_in.at[s, n - 1], z_to[n])
+
+    def z_end(s):
         sel, p = s // PARTS, s % PARTS
-        live[f"z2{s}"].wait()
-        g[p, sel] = f[s, b1].reshape(2, ROWS, 256)
-        got = decode(z2.at[s])
-        g[p, sel, 0] += got[0]
-        g[p, sel, 1] += got[1]
+        first, second = e[s, b1, b0, 0], e[s, b1, b0, 1]
+        for n in (1, 2, 3):
+            live[f"z{n}{s}"].wait()
+            got = decode(z_in.at[s, n - 1])
+            first, second = first + got[0], second + got[1]
+        g[p, sel, 0] = first
+        g[p, sel, 1] = second
 
         @pl.when(keep != sel)
         def _():
@@ -266,10 +269,7 @@
             def _():
                 copy(f"t{q}{p}", gsum.at[p, :, :, pl.ds(q * 128, 128)], rt.at[q, :, chunk(p)], t_to[q]).wait()
 
-    what = dict(
-        arrive=arrive, product=product, y_pass=y_pass, y_end=y_end, z_second=z_second, z_third=z_third,
-        last=last, finish=finish,
-    )
+    what = dict(arrive=arrive, product=product, y_pass=y_pass, y_end=y_end, z_end=z_end, last=last, finish=finish)
     for name, n in plan():
         what[name](n)
     d = jnp.transpose(drecv[...].reshape(128, 256))
@@ -288,12 +288,9 @@
             pltpu.VMEM((STAGES, 4, 8 * ROWS, 256), F32),
             pltpu.VMEM((STAGES, 6, WORDS, 2 * ROWS, 256), WORD),
             pltpu.VMEM((STAGES, 6, WORDS, 2 * ROWS, 256), WORD),
-            pltpu.VMEM((STAGES, 2, 2, 2 * ROWS, 256), F32),
-            pltpu.VMEM((STAGES, WORDS, 2 * ROWS, 256), WORD),
-            pltpu.VMEM((STAGES, WORDS, 2 * ROWS, 256), WORD),
-            pltpu.VMEM((STAGES, 2, 2 * ROWS, 256), F32),
-            pltpu.VMEM((STAGES, WORDS, ROWS, 256), WORD),
-            pltpu.VMEM((STAGES, WORDS, ROWS, 256), WORD),
+            pltpu.VMEM((STAGES, 2, 2, 2, ROWS, 256), F32),
+            pltpu.VMEM((STAGES, 3, WORDS, ROWS, 256), WORD),
+            pltpu.VMEM((STAGES, 3, WORDS, ROWS, 256), WORD),
             pltpu.VMEM((PARTS, 2, 2, ROWS, 256), F32),
             pltpu.VMEM((PARTS, WORDS, ROWS, 256), WORD),
             pltpu.VMEM((PARTS, WORDS, ROWS, 256), WORD),

time: 91.5 us -> 87.9 us (0.961)
  Pallas kernels: 88.3 us -> 84.6 us
    pallas_call x1, Pallas kernels: 88.3 us -> 84.6 us  [local(): pl.pallas_call(kernel, out_shape=jax.ShapeDtypeStruct((256, 128), jnp.bfl...]
where the time goes in v3:
time: 87.9 us; the launch traced here: 87.5 us
  Pallas kernels  84.6 us (96%)
  local copies, waits for them, and re-layouts  2.91 us (3%)
    pallas_call x1, Pallas kernels, local(): pl.pallas_call(kernel, out_shape=jax.ShapeDtypeStruct((256, 128), jnp.bfl...  84.6 us
    unnamed x4, local copies, waits for them, and re-layouts  1.99 us

profile of v3, /device:TPU:1, one launch (start us, length us, event | category | flops | bytes accessed | tf_op | source)
XLA Modules:
  0.0 87.5 jit_solution(18404174796815323021)
XLA Ops:
  0.0 0.0 copy-start
  0.0 1.0 %copy-done = bf16[4,2,64,384]{3,2,1,0:T(8,128)(2,1)S(1)} copy-done((bf16[4,2,64,384]{3,2,1,0:T(8,128)(2,1)S(1)}, bf16[4,2,64,384]{3,2,1,0:T(8,128)(2,1)}, u32[]{:S(2)}) %copy-start) | copy-done | bytes 393240
  1.0 0.0 copy-start.1
  1.0 1.0 %copy-done.1 = bf16[2,4,64,384]{3,2,1,0:T(8,128)(2,1)S(1)} copy-done((bf16[2,4,64,384]{3,2,1,0:T(8,128)(2,1)S(1)}, bf16[2,4,64,384]{3,2,1,0:T(8,128)(2,1)}, u32[]{:S(2)}) %copy-start.1) | copy-done | bytes 393240
  2.0 84.6 %shard_map.28 = bf16[256,128]{1,0:T(8,128)(2,1)S(1)} custom-call(bf16[4,2,64,384]{3,2,1,0:T(8,128)(2,1)S(1)} %copy-done, bf16[2,4,64,384]{3,2,1,0:T(8,128)(2,1)S(1)} %copy-done.1), custom_call_target="tpu_custom_call" | custom-call | tf_op jit(solution)/shard_map/pallas_call | solution.py:280
  86.6 0.1 reshape.6
  86.7 0.8 reshape.7
  (1 shorter events, 0.0 us)
Async XLA Ops:
  0.0 1.0 %copy-start = (bf16[4,2,64,384]{3,2,1,0:T(8,128)(2,1)S(1)}, bf16[4,2,64,384]{3,2,1,0:T(8,128)(2,1)}, u32[]{:S(2)}) copy-start(bf16[4,2,64,384]{3,2,1,0:T(8,128)(2,1)} %a_ref.1) | copy-start | bytes 1179652
  1.0 1.0 %copy-start.1 = (bf16[2,4,64,384]{3,2,1,0:T(8,128)(2,1)S(1)}, bf16[2,4,64,384]{3,2,1,0:T(8,128)(2,1)}, u32[]{:S(2)}) copy-start(bf16[2,4,64,384]{3,2,1,0:T(8,128)(2,1)} %w_ref.1) | copy-start | bytes 1179652

commit v4 on v3

--- a/solution.py
+++ b/solution.py
@@ -70,7 +70,7 @@
     return [(what, n) for _, what, n in sorted(steps, key=lambda step: step[0])]
 
 
-def kernel(a_ref, w_ref, o_ref, abuf, wbuf, t, y_out, y_in, e, z_out, z_in, g, z4_out, z4, gsum, drecv, rt, ss, rs, ls):
+def kernel(a_ref, w_ref, o_ref, abuf, wbuf, t, y_out, y_in, e, z_out, z_in, g, z4_out, z4, gsum, out, d_in, rt_in, drecv, rt, ss, rs, ls):
     ia, ja = lax.axis_index("ia"), lax.axis_index("ja")
     x, zh, c = ia // 4, (ia // 2) % 2, ia % 2
     y, zl = ja // 8, ja % 8
@@ -224,7 +224,7 @@
             copy(f"z4{p}", z4_out.at[p], z4.at[p], far).start()
 
     def swapped(p):
-        return copy(f"sw{p}", gsum.at[p], drecv.at[:, chunk(p)], swap)
+        return copy(f"sw{p}", out.at[p], d_in.at[p], swap)
 
     def last(p):
         copy(f"z4{p}", z4_out.at[p], z4.at[p], far).wait()
@@ -232,6 +232,8 @@
         gsum[p, 0] = g[p, keep, 0] + got[0]
         gsum[p, 1] = g[p, keep, 1] + got[1]
 
+        encode(out.at[p], gsum[p, 0], gsum[p, 1])
+
         @pl.when(stays)
         def _():
             drecv[:, chunk(p)] = gsum[p]
@@ -250,8 +252,8 @@
             @pl.when(jnp.logical_not(itself))
             def _():
                 pltpu.make_async_remote_copy(
-                    src_ref=gsum.at[p, :, :, pl.ds(q * 128, 128)],
-                    dst_ref=rt.at[b0, :, chunk(p)],
+                    src_ref=out.at[p, :, :, pl.ds(q * 128, 128)],
+                    dst_ref=rt_in.at[b0, p],
                     send_sem=ss.at[INDEX[f"t{q}{p}"]],
                     recv_sem=rs.at[INDEX[f"t0{p}"] + b0],
                     device_id=t_to[q],
@@ -262,12 +264,14 @@
         @pl.when(jnp.logical_not(stays))
         def _():
             swapped(p).wait()
+            drecv[0, chunk(p)], drecv[1, chunk(p)] = decode(d_in.at[p])
 
         for q in range(2):
 
             @pl.when(jnp.logical_not(jnp.logical_and(same, b0 == q)))
             def _():
-                copy(f"t{q}{p}", gsum.at[p, :, :, pl.ds(q * 128, 128)], rt.at[q, :, chunk(p)], t_to[q]).wait()
+                copy(f"t{q}{p}", out.at[p, :, :, pl.ds(q * 128, 128)], rt_in.at[q, p], t_to[q]).wait()
+                rt[q, 0, chunk(p)], rt[q, 1, chunk(p)] = decode(rt_in.at[q, p])
 
     what = dict(arrive=arrive, product=product, y_pass=y_pass, y_end=y_end, z_end=z_end, last=last, finish=finish)
     for name, n in plan():
@@ -295,6 +299,9 @@
             pltpu.VMEM((PARTS, WORDS, ROWS, 256), WORD),
             pltpu.VMEM((PARTS, WORDS, ROWS, 256), WORD),
             pltpu.VMEM((PARTS, 2, ROWS, 256), F32),
+            pltpu.VMEM((PARTS, WORDS, ROWS, 256), WORD),
+            pltpu.VMEM((PARTS, WORDS, ROWS, 256), WORD),
+            pltpu.VMEM((2, PARTS, WORDS, ROWS, 128), WORD),
             pltpu.VMEM((2, 64, 256), F32),
             pltpu.VMEM((2, 2, 64, 128), F32),
             pltpu.SemaphoreType.DMA((len(NAMES),)),

time: 87.9 us -> 87.8 us (level)
  no operation moved by 1% of the time
where the time goes in v4:
time: 87.8 us; the launch traced here: 87.4 us
  Pallas kernels  84.5 us (96%)
  local copies, waits for them, and re-layouts  2.91 us (3%)
    pallas_call x1, Pallas kernels, local(): pl.pallas_call(kernel, out_shape=jax.ShapeDtypeStruct((256, 128), jnp.bfl...  84.5 us
    unnamed x4, local copies, waits for them, and re-layouts  1.99 us

profile of v4, /device:TPU:1, one launch (start us, length us, event | category | flops | bytes accessed | tf_op | source)
XLA Modules:
  0.0 87.4 jit_solution(12812513322177938872)
XLA Ops:
  0.0 0.0 copy-start
  0.0 1.0 %copy-done = bf16[4,2,64,384]{3,2,1,0:T(8,128)(2,1)S(1)} copy-done((bf16[4,2,64,384]{3,2,1,0:T(8,128)(2,1)S(1)}, bf16[4,2,64,384]{3,2,1,0:T(8,128)(2,1)}, u32[]{:S(2)}) %copy-start) | copy-done | bytes 393240
  1.0 0.0 copy-start.1
  1.0 1.0 %copy-done.1 = bf16[2,4,64,384]{3,2,1,0:T(8,128)(2,1)S(1)} copy-done((bf16[2,4,64,384]{3,2,1,0:T(8,128)(2,1)S(1)}, bf16[2,4,64,384]{3,2,1,0:T(8,128)(2,1)}, u32[]{:S(2)}) %copy-start.1) | copy-done | bytes 393240
  2.0 84.5 %shard_map.28 = bf16[256,128]{1,0:T(8,128)(2,1)S(1)} custom-call(bf16[4,2,64,384]{3,2,1,0:T(8,128)(2,1)S(1)} %copy-done, bf16[2,4,64,384]{3,2,1,0:T(8,128)(2,1)S(1)} %copy-done.1), custom_call_target="tpu_custom_call" | custom-call | tf_op jit(solution)/shard_map/pallas_call | solution.py:284
  86.5 0.1 reshape.6
  86.6 0.8 reshape.7
  (1 shorter events, 0.0 us)
Async XLA Ops:
  0.0 1.0 %copy-start = (bf16[4,2,64,384]{3,2,1,0:T(8,128)(2,1)S(1)}, bf16[4,2,64,384]{3,2,1,0:T(8,128)(2,1)}, u32[]{:S(2)}) copy-start(bf16[4,2,64,384]{3,2,1,0:T(8,128)(2,1)} %a_ref.1) | copy-start | bytes 1179652
  1.0 1.0 %copy-start.1 = (bf16[2,4,64,384]{3,2,1,0:T(8,128)(2,1)S(1)}, bf16[2,4,64,384]{3,2,1,0:T(8,128)(2,1)}, u32[]{:S(2)}) copy-start(bf16[2,4,64,384]{3,2,1,0:T(8,128)(2,1)} %w_ref.1) | copy-start | bytes 1179652

commit v5 on v3

--- a/solution.py
+++ b/solution.py
@@ -144,10 +144,10 @@
     own_a.wait()
     own_w.wait()
     for name in ("w", "a1", "a2", "a3"):
-        live[name].wait()
+        live[name].wait_recv()
 
     def arrive(p):
-        live[f"cross{p}"].wait()
+        live[f"cross{p}"].wait_recv()
         if p + AHEAD < PARTS:
             start_cross(p + AHEAD)
         part = wbuf.at[1, c, :, :, chunk(p)]
@@ -158,7 +158,7 @@
     def product(s):
         sel, p = s // PARTS, s % PARTS
         if sel:
-            live[f"cf{p}"].wait()
+            live[f"cf{p}"].wait_recv()
 
         def one(n, _):
             total = None
@@ -185,7 +185,7 @@
         begin(f"y{n}{s}", y_out.at[s, n], y_in.at[s, n], target)
 
     def y_got(s, n):
-        live[f"y{n}{s}"].wait()
+        live[f"y{n}{s}"].wait_recv()
         return jnp.concatenate(decode(y_in.at[s, n]), axis=0)
 
     def y_pass(s):
@@ -212,7 +212,7 @@
         sel, p = s // PARTS, s % PARTS
         first, second = e[s, b1, b0, 0], e[s, b1, b0, 1]
         for n in (1, 2, 3):
-            live[f"z{n}{s}"].wait()
+            live[f"z{n}{s}"].wait_recv()
             got = decode(z_in.at[s, n - 1])
             first, second = first + got[0], second + got[1]
         g[p, sel, 0] = first
@@ -227,7 +227,7 @@
         return copy(f"sw{p}", gsum.at[p], drecv.at[:, chunk(p)], swap)
 
     def last(p):
-        copy(f"z4{p}", z4_out.at[p], z4.at[p], far).wait()
+        copy(f"z4{p}", z4_out.at[p], z4.at[p], far).wait_recv()
         got = decode(z4.at[p])
         gsum[p, 0] = g[p, keep, 0] + got[0]
         gsum[p, 1] = g[p, keep, 1] + got[1]
@@ -272,6 +272,10 @@
     what = dict(arrive=arrive, product=product, y_pass=y_pass, y_end=y_end, z_end=z_end, last=last, finish=finish)
     for name, n in plan():
         what[name](n)
+    for one in live.values():
+        one.wait_send()
+    for p in range(PARTS):
+        copy(f"z4{p}", z4_out.at[p], z4.at[p], far).wait_send()
     d = jnp.transpose(drecv[...].reshape(128, 256))
     o_ref[...] = (d + rt[...].reshape(256, 128)).astype(jnp.bfloat16)
 

time: 87.9 us -> 87.4 us (level)
  Pallas kernels: 84.6 us -> 83.5 us
    pallas_call x1, Pallas kernels: 84.6 us -> 83.5 us  [local(): pl.pallas_call(kernel, out_shape=jax.ShapeDtypeStruct((256, 128), jnp.bfl...]
where the time goes in v5:
time: 87.4 us; the launch traced here: 86.5 us
  Pallas kernels  83.5 us (96%)
  local copies, waits for them, and re-layouts  2.91 us (3%)
    pallas_call x1, Pallas kernels, local(): pl.pallas_call(kernel, out_shape=jax.ShapeDtypeStruct((256, 128), jnp.bfl...  83.5 us
    unnamed x4, local copies, waits for them, and re-layouts  1.99 us

profile of v5, /device:TPU:1, one launch (start us, length us, event | category | flops | bytes accessed | tf_op | source)
XLA Modules:
  0.0 86.5 jit_solution(14041989270046772553)
XLA Ops:
  0.0 0.0 copy-start
  0.0 1.0 %copy-done = bf16[4,2,64,384]{3,2,1,0:T(8,128)(2,1)S(1)} copy-done((bf16[4,2,64,384]{3,2,1,0:T(8,128)(2,1)S(1)}, bf16[4,2,64,384]{3,2,1,0:T(8,128)(2,1)}, u32[]{:S(2)}) %copy-start) | copy-done | bytes 393240
  1.0 0.0 copy-start.1
  1.0 1.0 %copy-done.1 = bf16[2,4,64,384]{3,2,1,0:T(8,128)(2,1)S(1)} copy-done((bf16[2,4,64,384]{3,2,1,0:T(8,128)(2,1)S(1)}, bf16[2,4,64,384]{3,2,1,0:T(8,128)(2,1)}, u32[]{:S(2)}) %copy-start.1) | copy-done | bytes 393240
  2.0 83.5 %shard_map.28 = bf16[256,128]{1,0:T(8,128)(2,1)S(1)} custom-call(bf16[4,2,64,384]{3,2,1,0:T(8,128)(2,1)S(1)} %copy-done, bf16[2,4,64,384]{3,2,1,0:T(8,128)(2,1)S(1)} %copy-done.1), custom_call_target="tpu_custom_call" | custom-call | tf_op jit(solution)/shard_map/pallas_call | solution.py:284
  85.5 0.1 reshape.6
  85.7 0.8 reshape.7
  (1 shorter events, 0.0 us)
Async XLA Ops:
  0.0 1.0 %copy-start = (bf16[4,2,64,384]{3,2,1,0:T(8,128)(2,1)S(1)}, bf16[4,2,64,384]{3,2,1,0:T(8,128)(2,1)}, u32[]{:S(2)}) copy-start(bf16[4,2,64,384]{3,2,1,0:T(8,128)(2,1)} %a_ref.1) | copy-start | bytes 1179652
  1.0 1.0 %copy-start.1 = (bf16[2,4,64,384]{3,2,1,0:T(8,128)(2,1)S(1)}, bf16[2,4,64,384]{3,2,1,0:T(8,128)(2,1)}, u32[]{:S(2)}) copy-start(bf16[2,4,64,384]{3,2,1,0:T(8,128)(2,1)} %w_ref.1) | copy-start | bytes 1179652
